TPU v7x, 32 devices: a whole 2x2x4 slice. The times are simulated.
32 devices in a mesh: groups: 2 (over x), wide: 8 (over z, y), narrow: 2 (over core).
Axes of the slice: x: 2, y: 2, z: 4, core: 2. Of those that a mesh axis runs over, the one named last changes fastest.
Arguments:
- tokens: bfloat16 [1024, 18432], P(('groups', 'narrow'), 'wide'), parts along dimension 0, may hold values from -6 to 6
- w_query: bfloat16 [18432, 7168], P('wide', 'narrow'), may hold values from -0.046875 to 0.046875
- w_keyval: bfloat16 [18432, 512], P('wide'), may hold values from -0.09375 to 0.09375
- cache_keys: bfloat16 [1024, 256, 256], P(('groups', 'wide')), parts along dimension 0, may hold values from -300 to 300
- cache_values: bfloat16 [1024, 256, 256], P(('groups', 'wide')), parts along dimension 0, may hold values from -24 to 24
- w_out: bfloat16 [7168, 18432], P('narrow', 'wide'), may hold values from -0.0625 to 0.0625
Outputs:
- attended: bfloat16 [1024, 18432], P(('groups', 'narrow'), 'wide'), parts along dimension 0
There are 2 independent parts, one for each index of `groups`. A program takes and returns all parts, laid end to end along the dimension named above; an argument that names none is the same for every part. Nothing has to cross between parts.
All inputs are finite; a program needn't handle non-finite values.
Results may differ from a plain program's by a relative error of at most 0.012.
The roundings to bfloat16 on the way count: a program that leaves them out, or rounds other values in their place, can miss the bound.
Values may be sent and summed in bfloat16 or wider, within the bound.
A program may use at most 192 MiB of HBM per device.

v0:
```python
import jax
import jax.numpy as jnp
from jax import lax
from jax.sharding import PartitionSpec as P


def attend(query, keyval, cache_keys, cache_values):
    head_size = cache_keys.shape[-1]
    local_rows = query.shape[0]
    local_heads = query.shape[1] // head_size
    heads_q = query.reshape(local_rows, local_heads, head_size)
    new_key = keyval[:, :head_size]
    new_value = keyval[:, head_size:]
    scale = head_size ** (-0.5)
    cached = (
        jnp.einsum("rhd,rld->rhl", heads_q, cache_keys, preferred_element_type=jnp.float32) * scale
    )
    own = jnp.einsum("rhd,rd->rh", heads_q, new_key, preferred_element_type=jnp.float32) * scale
    top = jnp.maximum(jnp.max(cached, axis=-1), own)
    cached_exp = jnp.exp(cached - top[:, :, None])
    own_exp = jnp.exp(own - top)
    total = jnp.sum(cached_exp, axis=-1) + own_exp
    probs_cached = (cached_exp / total[:, :, None]).astype(jnp.bfloat16)
    probs_own = (own_exp / total).astype(jnp.bfloat16)
    mixed = jnp.einsum(
        "rhl,rld->rhd", probs_cached, cache_values, preferred_element_type=jnp.float32
    )
    mixed = (
        mixed
        + probs_own.astype(jnp.float32)[:, :, None] * new_value.astype(jnp.float32)[:, None, :]
    )
    return mixed.astype(jnp.bfloat16).reshape(local_rows, local_heads * head_size)


def shards(tokens, w_query, w_keyval, cache_keys, cache_values, w_out):
    gathered = lax.all_gather(tokens, "narrow", axis=0, tiled=True)
    query_cols = w_query.shape[1]
    first = jnp.dot(gathered, w_query, preferred_element_type=jnp.float32)
    second = jnp.dot(gathered, w_keyval, preferred_element_type=jnp.float32)
    projected = lax.psum_scatter(
        jnp.concatenate([first, second], axis=1), "wide", scatter_dimension=0, tiled=True
    )
    projected = projected.astype(jnp.bfloat16)
    query = projected[:, :query_cols]
    keyval = projected[:, query_cols:]
    mixed = attend(query, keyval, cache_keys, cache_values)
    partial_out = jnp.dot(
        lax.all_gather(mixed, "wide", axis=0, tiled=True), w_out, preferred_element_type=jnp.float32
    )
    result = lax.psum_scatter(partial_out, "narrow", scatter_dimension=0, tiled=True)
    return result.astype(jnp.bfloat16)


def solution(mesh):
    in_specs = (
        P(("groups", "narrow"), "wide"),
        P("wide", "narrow"),
        P("wide", None),
        P(("groups", "wide"), None, None),
        P(("groups", "wide"), None, None),
        P("narrow", "wide"),
    )
    out_specs = P(("groups", "narrow"), "wide")
    return jax.shard_map(shards, mesh=mesh, in_specs=in_specs, out_specs=out_specs, check_vma=False)
```

profile of v0, /device:TPU:1, one launch (start us, length us, event | category | flops | bytes accessed | tf_op | source)
XLA Modules:
  0.0 313.2 jit_solution(254798748495817754)
XLA Ops:
  6.5 0.0 copy-start
  6.5 0.0 all-gather.3.cloned.1.call-start
  6.5 0.7 all-gather.3.cloned.1.call-update
  7.3 0.0 reduce-scatter.3.cloned.1.call-start
  7.3 15.1 %all-gather.3.cloned.1.call-done = bf16[512,2304]{1,0:T(8,128)(2,1)} async-done(((bf16[256,2304]{1,0:T(8,128)(2,1)}), bf16[512,2304]{1,0:T(8,128)(2,1)}) %all-gather.3.cloned.1.call-update) | async-done | bytes 2359312 | tf_op jit(solution)/shard_map/all_gather | solution.py:36
  22.4 0.0 copy-done
  22.4 0.0 copy-start.2
  22.4 3.2 %fusion.10 = f32[512,512]{1,0:T(8,128)S(1)} fusion(bf16[512,2304]{1,0:T(8,128)(2,1)} %all-gather.3.cloned.1.call-done, bf16[2304,512]{1,0:T(8,128)(2,1)S(1)} %copy-done), kind=kOutput, calls=%fused_computation.20 | convolution fusion | flops 1207959552 | bytes 5767168 | tf_op jit(solution)/shard_map/dot_general | solution.py:39
  25.6 0.0 copy-done.2
  25.6 14.2 %fusion.9 = f32[512,3584]{1,0:T(8,128)} fusion(bf16[512,2304]{1,0:T(8,128)(2,1)S(1)} %copy-done.2, bf16[2304,3584]{1,0:T(8,128)(2,1)} %param.7), kind=kOutput, calls=%fused_computation.19 | convolution fusion | flops 8455716864 | bytes 26214400 | tf_op jit(solution)/shard_map/dot_general | solution.py:38
  39.7 7.0 %pad_maximum_fusion = f32[512,4096]{1,0:T(8,128)} fusion(f32[512,512]{1,0:T(8,128)S(1)} %fusion.10, f32[512,3584]{1,0:T(8,128)} %fusion.9), kind=kLoop, calls=%fused_computation | loop fusion | flops 2097152 | bytes 16777216 | tf_op jit(solution)/shard_map/concatenate | solution.py:41
  46.8 0.0 reduce-scatter.3.cloned.1.call-update
  46.8 0.0 all-gather.5.cloned.1.call-start
  46.8 150.0 %reduce-scatter.3.cloned.1.call-done = f32[64,4096]{1,0:T(8,128)} async-done(((f32[512,4096]{1,0:T(8,128)}), f32[64,4096]{1,0:T(8,128)}) %reduce-scatter.3.cloned.1.call-update) | async-done | bytes 1048592 | tf_op jit(solution)/shard_map/reduce_scatter | solution.py:40
  196.8 1.3 convert_element_type.21
  198.2 0.3 reshape.10
  198.5 0.2 fusion.4
  198.7 5.8 %fusion.8 = (f32[64,14]{1,0:T(8,128)S(1)}, f32[64,14,256]{2,1,0:T(8,128)S(1)}) fusion(bf16[64,14,256]{2,1,0:T(8,128)(2,1)S(1)} %reshape.10, bf16[64,256,256]{2,1,0:T(8,128)(2,1)} %param.9), kind=kOutput, calls=%fused_computation.18 | convolution fusion | flops 117898368 | bytes 9768448 | tf_op jit(solution)/shard_map/rhd,rld->rhl/dot_general | solution.py:16
  204.5 0.4 fusion.1
  204.9 4.7 %fusion = bf16[64,14,256]{2,1,0:T(8,128)(2,1)S(1)} fusion(bf16[64,256,256]{2,1,0:T(8,128)(2,1)} %param.10, f32[64,14,256]{2,1,0:T(8,128)S(1)} %get-tuple-element.10, f32[64,256]{1,0:T(8,128)S(1)} %get-tuple-element.6, f32[64,14]{1,0:T(8,128)S(1)} %get-tuple-element.8, f32[64,14]{1,0:T(8,128)S(1)} %get-tuple-element.7, f32[64,14]{1,0:T(8,128)S(1)} %multiply_maximum_fusion), kind=kOutput, calls=%fused_computation.3 | convolution fusion | flops 118816768 | bytes 9841152 | tf_op jit(solution)/shard_map/rhl,rld->rhd/dot_general | solution.py:25
  209.6 0.9 copy.12
  210.5 0.0 all-gather.5.cloned.1.call-update
  210.6 0.0 reduce-scatter.5.cloned.1.call-start
  210.6 64.9 %all-gather.5.cloned.1.call-done = bf16[512,3584]{1,0:T(8,128)(2,1)} async-done(((bf16[64,3584]{1,0:T(8,128)(2,1)}), bf16[512,3584]{1,0:T(8,128)(2,1)}) %all-gather.5.cloned.1.call-update) | async-done | bytes 3670032 | tf_op jit(solution)/shard_map/all_gather | solution.py:48
  275.5 0.0 copy-start.1
  275.5 15.8 %fusion.11 = f32[512,2304]{1,0:T(8,128)} fusion(bf16[512,3584]{1,0:T(8,128)(2,1)} %all-gather.5.cloned.1.call-done, bf16[3584,2304]{1,0:T(8,128)(2,1)} %param.11), kind=kOutput, calls=%fused_computation.21 | convolution fusion | flops 8455716864 | bytes 24903680 | tf_op jit(solution)/shard_map/dot_general | solution.py:47
  291.3 0.0 reduce-scatter.5.cloned.1.call-update
  291.3 12.6 %reduce-scatter.5.cloned.1.call-done = f32[256,2304]{1,0:T(8,128)} async-done(((f32[512,2304]{1,0:T(8,128)}), f32[256,2304]{1,0:T(8,128)}) %reduce-scatter.5.cloned.1.call-update) | async-done | bytes 2359312 | tf_op jit(solution)/shard_map/reduce_scatter | solution.py:50
  303.9 2.8 convert_element_type.27
  306.7 0.0 copy-done.1
  (4 shorter events, 0.1 us)
Async XLA Ops:
  6.5 15.8 %copy-start = (bf16[2304,512]{1,0:T(8,128)(2,1)S(1)}, bf16[2304,512]{1,0:T(8,128)(2,1)}, u32[]{:S(2)}) copy-start(bf16[2304,512]{1,0:T(8,128)(2,1)} %param.8) | copy-start | bytes 7077892
  6.5 15.8 %all-gather.3.cloned.1.call-start = ((), (), s32[]{:S(2)}) async-start(), calls=%async_computation.2 | async-start | bytes 3538944 | tf_op jit(solution)/shard_map/all_gather | solution.py:36
  7.3 189.6 %reduce-scatter.3.cloned.1.call-start = ((), (), s32[]{:S(2)}) async-start(), calls=%async_computation.3 | async-start | bytes 9437184 | tf_op jit(solution)/shard_map/reduce_scatter | solution.py:40
  22.4 3.2 %copy-start.2 = (bf16[512,2304]{1,0:T(8,128)(2,1)S(1)}, bf16[512,2304]{1,0:T(8,128)(2,1)}, u32[]{:S(2)}) copy-start(bf16[512,2304]{1,0:T(8,128)(2,1)} %all-gather.3.cloned.1.call-done) | copy-start | bytes 7077892
  46.8 228.7 %all-gather.5.cloned.1.call-start = ((), (), s32[]{:S(2)}) async-start(), calls=%async_computation.4 | async-start | bytes 4128768 | tf_op jit(solution)/shard_map/all_gather | solution.py:48
  210.6 93.3 %reduce-scatter.5.cloned.1.call-start = ((), (), s32[]{:S(2)}) async-start(), calls=%async_computation.5 | async-start | bytes 7077888 | tf_op jit(solution)/shard_map/reduce_scatter | solution.py:50
  275.5 31.2 %copy-start.1 = (bf16[2304,512]{1,0:T(8,128)(2,1)S(1)}, bf16[2304,512]{1,0:T(8,128)(2,1)}, u32[]{:S(2)}) copy-start(bf16[2304,512]{1,0:T(8,128)(2,1)} %param.8) | copy-start | bytes 7077892
Sparse Core Ops, SparseCore 0:
  8.9 13.4 all-gather.2
  46.9 149.8 reduce-scatter.2
  210.7 64.7 all-gather.4
  291.4 12.4 reduce-scatter.4
where the time goes:
time: 314 us; the launch traced here: 313 us
  waiting for transfers between devices  243 us (77%)
  matrix products  43.8 us (14%)
  between operations  13.2 us (4%)
  other arithmetic  11.5 us (4%)
    reduce_scatter x1, waiting for transfers between devices, shards(): lax.psum_scatter(jnp.concatenate([first, second], axis=1), 'wide', scatte...  150 us
    all_gather x1, waiting for transfers between devices, shards(): lax.all_gather(mixed, 'wide', axis=0, tiled=True)  64.9 us
    dot_general x1, matrix products, shards(): jnp.dot(lax.all_gather(mixed, 'wide', axis=0, tiled=True), w_out, preferr...  15.8 us
    all_gather x1, waiting for transfers between devices, shards(): gathered = lax.all_gather(tokens, 'narrow', axis=0, tiled=True)  15.1 us
    dot_general x1, matrix products, shards(): first = jnp.dot(gathered, w_query, preferred_element_type=jnp.float32)  14.2 us
    reduce_scatter x1, waiting for transfers between devices, shards(): lax.psum_scatter(partial_out, 'narrow', scatter_dimension=0, tiled=True)  12.6 us
    concatenate x1, other arithmetic, shards(): jnp.concatenate([first, second], axis=1)  7.03 us
  transfers between devices with their start and end apart: 4, of which 4 were waited for; matrix products, arithmetic and copies ran while one was open for 0% of the time, Pallas kernels for 0%

commit v1 on v0

v1 whole, which is shorter than its diff:
```python
import functools
import math

import jax
import jax.numpy as jnp
from jax import lax
from jax.experimental import pallas as pl
from jax.experimental.pallas import tpu as pltpu
from jax.sharding import PartitionSpec as P

MESH = pl.DeviceIdType.MESH
F32 = jnp.float32
BF16 = jnp.bfloat16
LAG = 3
BLOCK = 128


def bound_shift(width):
    return 15 - math.ceil(math.log2(2 * width * 6.0 * 0.09375))


def encode(x, shift):
    x = x * 2.0**shift
    x2 = x * x
    x4 = x2 * x2
    x8 = x4 * x4
    return jnp.where(x < 0, -x8, x8).astype(BF16)


def decode(y, shift):
    y = y.astype(F32)
    x = jnp.exp2(jnp.log2(jnp.abs(y)) * 0.125 - shift)
    return jnp.where(y < 0, -x, x)


def wait_bytes(ref, sem):
    pltpu.make_async_copy(ref, ref, sem).wait()


def peers(wide):
    outers = wide // 2
    me = lax.axis_index("wide")
    outer, inner = me // 2, me % 2
    partner = outer * 2 + 1 - inner
    others = [lax.rem(outer + k, outers) for k in range(1, outers)]
    return outers, me, outer, inner, partner, others


def greet(wide):
    outers, _, _, inner, partner, others = peers(wide)
    barrier = pltpu.get_barrier_semaphore()
    pl.semaphore_signal(barrier, inc=1, device_id={"narrow": 1 - lax.axis_index("narrow")}, device_id_type=MESH)
    pl.semaphore_signal(barrier, inc=1, device_id={"wide": partner}, device_id_type=MESH)
    for other in others:
        pl.semaphore_signal(barrier, inc=1, device_id={"wide": other * 2 + inner}, device_id_type=MESH)
    pl.semaphore_wait(barrier, 1 + outers)


def remote(src, dst, send, recv, where):
    return pltpu.make_async_remote_copy(
        src_ref=src, dst_ref=dst, send_sem=send, recv_sem=recv, device_id=where, device_id_type=MESH
    )


def project_kernel(
    wide, dh, tokens, w_query, w_keyval, query, keyval,
    tok, weights, product, mine, kept, pair_out, pair_in, line_out, line_in, new,
    w_sem, tok_sem, pair_send, pair_recv, line_send, line_recv, new_sem,
):
    outers, _, outer, inner, partner, others = peers(wide)
    half = lax.axis_index("narrow")
    chunks, rows = pair_out.shape[0], kept.shape[1]
    heads = chunks - 1
    width = tokens.shape[1]
    shift = bound_shift(width)

    def head_copy(h):
        columns = pl.ds(pl.multiple_of(h * dh, dh), dh)
        return pltpu.make_async_copy(w_query.at[:, columns], weights.at[h + 1], w_sem.at[h + 1])

    own_tokens = pltpu.make_async_copy(tokens, tok.at[half], tok_sem.at[0])
    own_tokens.start()
    columns = pl.ds(pl.multiple_of(half * dh, dh), dh)
    pltpu.make_async_copy(w_keyval.at[:, columns], weights.at[0], w_sem.at[0]).start()
    greet(wide)
    across = {"narrow": 1 - half}
    pair_tokens = remote(tokens, tok.at[half], tok_sem.at[1], tok_sem.at[2], across)
    pair_tokens.start()

    @pl.loop(0, heads)
    def _(h):
        head_copy(h).start()

    own_tokens.wait()
    pair_tokens.wait_recv()

    def pair_copy(c):
        return remote(pair_out.at[c], pair_in.at[c], pair_send, pair_recv.at[c], {"wide": partner})

    @pl.loop(0, chunks + 2 * LAG)
    def _(t):
        @pl.when(t < chunks)
        def _():
            wait_bytes(weights.at[t], w_sem.at[t])
            product[...] = jnp.dot(
                tok[...].reshape(wide * rows, width), weights[t], preferred_element_type=F32
            ).reshape(wide, rows, dh)
            for o in range(outers):
                pair_out[t, o] = encode(product[2 * o + 1 - inner], shift)
                mine[t, o] = product[2 * o + inner]
            pair_copy(t).start()

        @pl.when(jnp.logical_and(t >= LAG, t < chunks + LAG))
        def _():
            c = t - LAG
            wait_bytes(pair_in.at[c], pair_recv.at[c])
            for k, other in enumerate(others):
                line_out[c, k] = encode(mine[c, other] + decode(pair_in[c, other], shift), shift)
                remote(
                    line_out.at[c, k], line_in.at[c, k], line_send, line_recv.at[c], {"wide": other * 2 + inner}
                ).start()
            kept[c] = mine[c, outer] + decode(pair_in[c, outer], shift)

        @pl.when(t >= 2 * LAG)
        def _():
            c = t - 2 * LAG
            wait_bytes(line_in.at[c], line_recv.at[c])
            total = kept[c]
            for k in range(outers - 1):
                total += decode(line_in[c, k], shift)
            total = total.astype(BF16)

            @pl.when(c == 0)
            def _():
                new[half] = total
                remote(new.at[half], new.at[half], new_sem.at[0], new_sem.at[1], across).start()

            @pl.when(c > 0)
            def _():
                query[:, pl.ds(pl.multiple_of((c - 1) * dh, dh), dh)] = total

    pair_tokens.wait_send()
    new_copy = remote(new.at[half], new.at[half], new_sem.at[0], new_sem.at[1], across)
    new_copy.wait_recv()
    keyval[:, :dh] = new[0]
    keyval[:, dh:] = new[1]
    new_copy.wait_send()
    wait_bytes(pair_out, pair_send)
    wait_bytes(line_out, line_send)


def project(wide, dh, tokens, w_query, w_keyval):
    width = tokens.shape[1]
    total_rows = 2 * tokens.shape[0]
    rows = total_rows // wide
    outers = wide // 2
    heads = w_query.shape[1] // dh
    chunks = heads + 1
    dma = pltpu.SemaphoreType.DMA
    return pl.pallas_call(
        functools.partial(project_kernel, wide, dh),
        out_shape=[
            jax.ShapeDtypeStruct((rows, heads * dh), BF16),
            jax.ShapeDtypeStruct((rows, 2 * dh), BF16),
        ],
        in_specs=[pl.BlockSpec(memory_space=pl.ANY)] * 3,
        out_specs=[pl.BlockSpec(memory_space=pltpu.VMEM)] * 2,
        scratch_shapes=[
            pltpu.VMEM((2, total_rows // 2, width), BF16),
            pltpu.VMEM((chunks, width, dh), BF16),
            pltpu.VMEM((wide, rows, dh), F32),
            pltpu.VMEM((chunks, outers, rows, dh), F32),
            pltpu.VMEM((chunks, rows, dh), F32),
            pltpu.VMEM((chunks, outers, rows, dh), BF16),
            pltpu.VMEM((chunks, outers, rows, dh), BF16),
            pltpu.VMEM((chunks, outers - 1, rows, dh), BF16),
            pltpu.VMEM((chunks, outers - 1, rows, dh), BF16),
            pltpu.VMEM((2, rows, dh), BF16),
            dma((chunks,)),
            dma((3,)),
            dma,
            dma((chunks,)),
            dma,
            dma((chunks,)),
            dma((2,)),
        ],
        compiler_params=pltpu.CompilerParams(
            collective_id=0, has_side_effects=True, vmem_limit_bytes=60 * 2**20
        ),
        cost_estimate=pl.CostEstimate(
            flops=2 * total_rows * width * chunks * dh, bytes_accessed=2 * width * chunks * dh, transcendentals=0
        ),
    )(tokens, w_query, w_keyval)


def output_kernel(
    wide, mixed, w_out, result,
    gathered, weights, total, half_out, half_in,
    w_sem, send, line_recv, pair_recv, half_send, half_recv,
):
    outers, me, _, inner, partner, others = peers(wide)
    half = lax.axis_index("narrow")
    chunks, _, rows, cols = gathered.shape
    blocks = half_out.shape[0]

    @pl.loop(0, chunks)
    def _(g):
        pltpu.make_async_copy(
            w_out.at[pl.ds(pl.multiple_of(g * cols, cols), cols), :], weights.at[g], w_sem.at[g]
        ).start()
        gathered[g, me] = mixed[:, pl.ds(pl.multiple_of(g * cols, cols), cols)]

    greet(wide)

    def spread(g, block, where, recv):
        remote(gathered.at[g, block], gathered.at[g, block], send, recv, {"wide": where}).start()

    @pl.loop(0, chunks)
    def _(g):
        for other in others:
            spread(g, me, other * 2 + inner, line_recv.at[g])
        spread(g, me, partner, pair_recv.at[g])

    total[...] = jnp.zeros_like(total)

    def product(g, b):
        per = BLOCK // rows
        left = gathered[g, pl.ds(b * per, per)].reshape(BLOCK, cols)
        return jnp.dot(left, weights[g], preferred_element_type=F32)

    def arrive(g):
        wait_bytes(gathered.at[g, pl.ds(0, outers)], pair_recv.at[g])
        wait_bytes(weights.at[g], w_sem.at[g])

    @pl.loop(0, chunks)
    def _(g):
        wait_bytes(gathered.at[g, pl.ds(0, outers - 1)], line_recv.at[g])
        for other in others:
            spread(g, other * 2 + inner, partner, pair_recv.at[g])

        @pl.when(g > 0)
        def _():
            arrive(g - 1)

            @pl.loop(0, 2 * blocks)
            def _(b):
                total[b] += product(g - 1, b)

    last = chunks - 1
    arrive(last)

    def half_copy(b):
        return remote(half_out.at[b], half_in.at[b], half_send, half_recv.at[b], {"narrow": 1 - half})

    @pl.loop(0, blocks)
    def _(b):
        at = (1 - half) * blocks + b
        half_out[b] = (total[at] + product(last, at)).astype(BF16)
        half_copy(b).start()

    @pl.loop(0, blocks)
    def _(b):
        at = half * blocks + b
        own = total[at] + product(last, at)
        wait_bytes(half_in.at[b], half_recv.at[b])
        result[b] = (own + half_in[b].astype(F32)).astype(BF16)

    wait_bytes(half_out, half_send)
    wait_bytes(gathered.at[:, pl.ds(0, 2 * outers - 1)], send)


def project_out(wide, mixed, w_out):
    rows, features = mixed.shape
    width = w_out.shape[1]
    cols = 512
    chunks = features // cols
    blocks = wide * rows // 2 // BLOCK
    dma = pltpu.SemaphoreType.DMA
    result = pl.pallas_call(
        functools.partial(output_kernel, wide),
        out_shape=jax.ShapeDtypeStruct((blocks, BLOCK, width), BF16),
        in_specs=[pl.BlockSpec(memory_space=pltpu.VMEM), pl.BlockSpec(memory_space=pl.ANY)],
        out_specs=pl.BlockSpec(memory_space=pltpu.VMEM),
        scratch_shapes=[
            pltpu.VMEM((chunks, wide, rows, cols), BF16),
            pltpu.VMEM((chunks, cols, width), BF16),
            pltpu.VMEM((2 * blocks, BLOCK, width), F32),
            pltpu.VMEM((blocks, BLOCK, width), BF16),
            pltpu.VMEM((blocks, BLOCK, width), BF16),
            dma((chunks,)),
            dma,
            dma((chunks,)),
            dma((chunks,)),
            dma,
            dma((blocks,)),
        ],
        compiler_params=pltpu.CompilerParams(
            collective_id=1, has_side_effects=True, vmem_limit_bytes=60 * 2**20
        ),
        cost_estimate=pl.CostEstimate(
            flops=2 * wide * rows * features * width, bytes_accessed=2 * features * width, transcendentals=0
        ),
    )(mixed, w_out)
    return result.reshape(blocks * BLOCK, width)


def attend(query, keyval, cache_keys, cache_values):
    head_size = cache_keys.shape[-1]
    local_rows = query.shape[0]
    local_heads = query.shape[1] // head_size
    heads_q = query.reshape(local_rows, local_heads, head_size)
    new_key = keyval[:, :head_size]
    new_value = keyval[:, head_size:]
    scale = head_size ** (-0.5)
    cached = (
        jnp.einsum("rhd,rld->rhl", heads_q, cache_keys, preferred_element_type=jnp.float32) * scale
    )
    own = jnp.einsum("rhd,rd->rh", heads_q, new_key, preferred_element_type=jnp.float32) * scale
    top = jnp.maximum(jnp.max(cached, axis=-1), own)
    cached_exp = jnp.exp(cached - top[:, :, None])
    own_exp = jnp.exp(own - top)
    total = jnp.sum(cached_exp, axis=-1) + own_exp
    probs_cached = (cached_exp / total[:, :, None]).astype(jnp.bfloat16)
    probs_own = (own_exp / total).astype(jnp.bfloat16)
    mixed = jnp.einsum(
        "rhl,rld->rhd", probs_cached, cache_values, preferred_element_type=jnp.float32
    )
    mixed = (
        mixed
        + probs_own.astype(jnp.float32)[:, :, None] * new_value.astype(jnp.float32)[:, None, :]
    )
    return mixed.astype(jnp.bfloat16).reshape(local_rows, local_heads * head_size)


def shards(wide, tokens, w_query, w_keyval, cache_keys, cache_values, w_out):
    query, keyval = project(wide, cache_keys.shape[-1], tokens, w_query, w_keyval)
    mixed = attend(query, keyval, cache_keys, cache_values)
    return project_out(wide, mixed, w_out)


def solution(mesh):
    in_specs = (
        P(("groups", "narrow"), "wide"),
        P("wide", "narrow"),
        P("wide", None),
        P(("groups", "wide"), None, None),
        P(("groups", "wide"), None, None),
        P("narrow", "wide"),
    )
    out_specs = P(("groups", "narrow"), "wide")
    return jax.shard_map(
        functools.partial(shards, mesh.shape["wide"]),
        mesh=mesh, in_specs=in_specs, out_specs=out_specs, check_vma=False,
    )
```

time: 314 us -> 130 us (0.41)
  waiting for transfers between devices: 243 us -> 0 us
  Pallas kernels: 0 us -> 116 us
  matrix products: 43.8 us -> 7.62 us
  between operations: 13.2 us -> 0.06 us
  other arithmetic: 11.5 us -> 1.33 us
  local copies, waits for them, and re-layouts: 1.32 us -> 4.66 us
    reduce_scatter x2 -> x0, waiting for transfers between devices: 163 us -> none  [the longest x1 150 us: shards(): lax.psum_scatter(jnp.concatenate([first, second], axis=1), 'wide', scatte...]
    pallas_call x0 -> x2, Pallas kernels: none -> 116 us  [the longest x1 57.9 us: project(): pl.pallas_call(functools.partial(project_kernel, wide, dh), out_shape=[ja...]
    all_gather x2 -> x0, waiting for transfers between devices: 79.9 us -> none  [the longest x1 64.9 us: shards(): lax.all_gather(mixed, 'wide', axis=0, tiled=True)]
    dot_general x3 -> x0, matrix products: 33.2 us -> none  [the longest x1 15.8 us: shards(): jnp.dot(lax.all_gather(mixed, 'wide', axis=0, tiled=True), w_out, preferr...]
    concatenate x1 -> x0, other arithmetic: 7.03 us -> none  [shards(): jnp.concatenate([first, second], axis=1)]
    convert_element_type x2 -> x0, other arithmetic: 4.07 us -> none  [the longest x1 2.8 us: shards(): return result.astype(jnp.bfloat16)]
    dot_general x1, matrix products: 4.68 us -> 1.35 us  [attend(): jnp.einsum('rhl,rld->rhd', probs_cached, cache_values, preferred_element_...]
  transfers between devices with their start and end apart: 4 -> 0, of which waited for: 4 -> 0; matrix products, arithmetic and copies ran while one was open for 0% -> 0% of each run, Pallas kernels for 0% -> 0%
where the time goes in v1:
time: 130 us; the launch traced here: 129 us
  Pallas kernels  116 us (89%)
  matrix products  7.62 us (6%)
  local copies, waits for them, and re-layouts  4.66 us (4%)
  other arithmetic  1.33 us (1%)
    pallas_call x1, Pallas kernels, project(): pl.pallas_call(functools.partial(project_kernel, wide, dh), out_shape=[ja...  57.9 us
    pallas_call x1, Pallas kernels, project_out(): pl.pallas_call(functools.partial(output_kernel, wide), out_shape=jax.Shap...  57.7 us
    dot_general x1, matrix products, attend(): jnp.einsum('rhd,rld->rhl', heads_q, cache_keys, preferred_element_type=jn...  6.04 us
    unnamed x4, local copies, waits for them, and re-layouts  3.29 us

profile of v1, /device:TPU:1, one launch (start us, length us, event | category | flops | bytes accessed | tf_op | source)
XLA Modules:
  0.0 129.3 jit_solution(11694817826113889597)
XLA Ops:
  0.0 57.9 %shard_map.64 = (bf16[64,3584]{1,0:T(8,128)(2,1)}, bf16[64,512]{1,0:T(8,128)(2,1)}) custom-call(bf16[256,2304]{1,0:T(8,128)(2,1)} %tokens.1, bf16[2304,3584]{1,0:T(8,128)(2,1)} %w_query.1, bf16[2304,512]{1,0:T(8,128)(2,1)} %w_keyval.1), custom_call_target="tpu_custom_call" | custom-call | flops 9059696640 | bytes 17694720 | tf_op jit(solution)/shard_map/pallas_call | solution.py:160
  57.9 1.4 %reshape.13 = bf16[64,14,256]{2,1,0:T(8,128)(2,1)S(1)} reshape(bf16[64,3584]{1,0:T(8,128)(2,1)} %get-tuple-element.7) | data formatting | bytes 917504 | tf_op jit(solution)/shard_map/reshape | solution.py:311
  59.3 0.0 copy-start
  59.3 0.9 slice_bitcast_fusion
  60.2 0.2 fusion.4
  60.5 6.0 %fusion.8 = (f32[64,14]{1,0:T(8,128)S(1)}, f32[64,14,256]{2,1,0:T(8,128)S(1)}) fusion(bf16[64,14,256]{2,1,0:T(8,128)(2,1)S(1)} %reshape.13, bf16[64,256,256]{2,1,0:T(8,128)(2,1)} %param.9), kind=kOutput, calls=%fused_computation.17 | convolution fusion | flops 117898368 | bytes 9768448 | tf_op jit(solution)/shard_map/rhd,rld->rhl/dot_general | solution.py:316
  66.5 0.4 fusion.1
  66.9 0.0 copy-done
  66.9 1.3 %fusion = bf16[64,14,256]{2,1,0:T(8,128)(2,1)S(1)} fusion(bf16[64,256,256]{2,1,0:T(8,128)(2,1)S(1)} %copy-done, f32[64,14,256]{2,1,0:T(8,128)S(1)} %get-tuple-element.14, f32[64,256]{1,0:T(8,128)S(1)} %get-tuple-element.12, f32[64,14]{1,0:T(8,128)S(1)} %get-tuple-element.10, f32[64,14]{1,0:T(8,128)S(1)} %get-tuple-element.9, ...), kind=kOutput, calls=%fused_computation.2 | convolution fusion | flops 118816768 | bytes 9841152 | tf_op jit(solution)/shard_map/rhl,rld->rhd/dot_general | solution.py:325
  68.3 0.9 copy.9
  69.2 57.7 %shard_map.65 = bf16[2,128,2304]{2,1,0:T(8,128)(2,1)} custom-call(bf16[64,3584]{1,0:T(8,128)(2,1)} %bitcast.13, bf16[3584,2304]{1,0:T(8,128)(2,1)} %w_out.1), custom_call_target="tpu_custom_call" | custom-call | flops 8455716864 | bytes 16515072 | tf_op jit(solution)/shard_map/pallas_call | solution.py:279
  126.9 2.4 %copy.13 = bf16[256,2304]{1,0:T(8,128)(2,1)} copy(bf16[256,2304]{1,0:T(8,128)(2,1)} %bitcast.12) | data formatting | bytes 2359296
  (2 shorter events, 0.0 us)
Async XLA Ops:
  59.3 7.6 %copy-start = (bf16[64,256,256]{2,1,0:T(8,128)(2,1)S(1)}, bf16[64,256,256]{2,1,0:T(8,128)(2,1)}, u32[]{:S(2)}) copy-start(bf16[64,256,256]{2,1,0:T(8,128)(2,1)} %param.10) | copy-start | bytes 25165828

commit v2 on v0

v2 whole, which is shorter than its diff:
```python
import functools
import math

import jax
import jax.numpy as jnp
from jax import lax
from jax.experimental import pallas as pl
from jax.experimental.pallas import tpu as pltpu
from jax.sharding import PartitionSpec as P

MESH = pl.DeviceIdType.MESH
F32 = jnp.float32
BF16 = jnp.bfloat16
LAG = 3
SLOTS = LAG + 1
BLOCK = 128
GROUP = 8
BATCH = 8
AHEAD = 3


def bound_shift(width):
    return 15 - math.ceil(math.log2(2 * width * 6.0 * 0.09375))


def encode(x, shift, squarings):
    power = x * 2.0**shift
    for _ in range(squarings):
        power = power * power
    return jnp.where(x < 0, -power, power).astype(BF16)


def decode(y, shift, squarings):
    y = y.astype(F32)
    x = jnp.exp2(jnp.log2(jnp.abs(y)) * 0.5**squarings - shift)
    return jnp.where(y < 0, -x, x)


def wait_bytes(ref, sem):
    pltpu.make_async_copy(ref, ref, sem).wait()


def peers(wide):
    outers = wide // 2
    me = lax.axis_index("wide")
    outer, inner = me // 2, me % 2
    partner = outer * 2 + 1 - inner
    others = [lax.rem(outer + k, outers) for k in range(1, outers)]
    return outers, me, outer, inner, partner, others


def greet(wide):
    outers, _, _, inner, partner, others = peers(wide)
    barrier = pltpu.get_barrier_semaphore()
    pl.semaphore_signal(barrier, inc=1, device_id={"narrow": 1 - lax.axis_index("narrow")}, device_id_type=MESH)
    pl.semaphore_signal(barrier, inc=1, device_id={"wide": partner}, device_id_type=MESH)
    for other in others:
        pl.semaphore_signal(barrier, inc=1, device_id={"wide": other * 2 + inner}, device_id_type=MESH)
    pl.semaphore_wait(barrier, 1 + outers)


def remote(src, dst, send, recv, where):
    return pltpu.make_async_remote_copy(
        src_ref=src, dst_ref=dst, send_sem=send, recv_sem=recv, device_id=where, device_id_type=MESH
    )


def block_kernel(
    wide, tokens, w_query, w_keyval, cache_keys, cache_values, w_out, result,
    tok, weights, product, mine, kept, pair_out, pair_in, line_out, line_in, new, new_wide,
    query, mixed, keys, values, gathered, out_weights, total, half_out, half_in,
    w_sem, tok_sem, cache_sem, pair_send, pair_recv, line_send, line_recv, new_sem,
    out_sem, spread_send, spread_line, spread_pair, half_send, half_recv,
):
    outers, me, outer, inner, partner, others = peers(wide)
    half = lax.axis_index("narrow")
    across = {"narrow": 1 - half}
    chunks, _, rows, dh = pair_out.shape
    heads = chunks - 1
    width = tokens.shape[1]
    shift = bound_shift(width)
    scale = dh**-0.5
    pieces, cols = gathered.shape[0], gathered.shape[3]
    blocks = half_out.shape[0]
    batches = rows // BATCH
    first_heads = min(GROUP, heads)
    rest_heads = heads - first_heads
    begin = first_heads + 2 * LAG + 1
    per = -(-batches // 3)

    def weight_copy(c, slot):
        columns = pl.ds(pl.multiple_of((c - 1) * dh, dh), dh)
        return pltpu.make_async_copy(w_query.at[:, columns], weights.at[slot], w_sem.at[slot])

    def out_copy(g):
        take = pl.ds(pl.multiple_of(g * cols, cols), cols)
        slot = g % AHEAD
        return pltpu.make_async_copy(w_out.at[take, :], out_weights.at[slot], out_sem.at[slot])

    own_tokens = pltpu.make_async_copy(tokens, tok.at[half], tok_sem.at[0])
    own_tokens.start()
    columns = pl.ds(pl.multiple_of(half * dh, dh), dh)
    pltpu.make_async_copy(w_keyval.at[:, columns], weights.at[0], w_sem.at[0]).start()
    greet(wide)
    pair_tokens = remote(tokens, tok.at[half], tok_sem.at[1], tok_sem.at[2], across)
    pair_tokens.start()

    @pl.loop(1, SLOTS)
    def _(c):
        weight_copy(c, c).start()

    key_copy = pltpu.make_async_copy(cache_keys, keys, cache_sem.at[0])
    value_copy = pltpu.make_async_copy(cache_values, values, cache_sem.at[1])
    query[...] = jnp.zeros_like(query)
    own_tokens.wait()
    pair_tokens.wait_recv()

    new_copy = remote(new.at[half], new.at[half], new_sem.at[0], new_sem.at[1], across)

    def spread(g, block, where, recv):
        remote(
            gathered.at[g, block], gathered.at[g, block], spread_send, recv, {"wide": where}
        ).start()

    def forward(g):
        wait_bytes(gathered.at[g, pl.ds(0, outers - 1)], spread_line.at[g])
        for other in others:
            spread(g, other * 2 + inner, partner, spread_pair.at[g])

    def attend(group, b):
        take = pl.ds(pl.multiple_of(b * BATCH, BATCH), BATCH)
        q = query[group, take]
        cached = lax.dot_general(
            q.astype(BF16), keys[take], (((2,), (2,)), ((0,), (0,))), preferred_element_type=F32
        ) * scale
        new_key = new_wide[0, take][:, None, :]
        new_value = new_wide[1, take][:, None, :]
        own = jnp.sum(q * new_key, axis=-1, keepdims=True) * scale
        top = jnp.maximum(jnp.max(cached, axis=-1, keepdims=True), own)
        cached_exp = jnp.exp(cached - top)
        own_exp = jnp.exp(own - top)
        denominator = jnp.sum(cached_exp, axis=-1, keepdims=True) + own_exp
        probs = (cached_exp / denominator).astype(BF16)
        probs_own = (own_exp / denominator).astype(BF16).astype(F32)
        out = lax.dot_general(
            probs, values[take], (((2,), (1,)), ((0,), (0,))), preferred_element_type=F32
        )
        mixed[take] = out + probs_own * new_value

    def spread_group(first, count):
        for j in range(count):
            piece, at = divmod((first + j) * dh, cols)
            gathered[piece, me, :, at : at + dh] = mixed[:, j, :].astype(BF16)
        for g in range(first * dh // cols, (first + count) * dh // cols):
            for other in others:
                spread(g, me, other * 2 + inner, spread_line.at[g])
            spread(g, me, partner, spread_pair.at[g])

    @pl.loop(0, max(chunks + 2 * LAG, begin + 3))
    def _(t):
        @pl.when(t < chunks)
        def _():
            slot = t % SLOTS
            wait_bytes(weights.at[slot], w_sem.at[slot])
            product[...] = jnp.dot(
                tok[...].reshape(wide * rows, width), weights[slot], preferred_element_type=F32
            ).reshape(wide, rows, dh)
            for o in range(outers):
                pair_out[t, o] = encode(product[2 * o + 1 - inner], shift, 3)
                mine[slot, o] = product[2 * o + inner]
            remote(pair_out.at[t], pair_in.at[t], pair_send, pair_recv.at[t], {"wide": partner}).start()

            @pl.when(t + SLOTS < chunks)
            def _():
                weight_copy(t + SLOTS, slot).start()

        @pl.when(t == LAG)
        def _():
            key_copy.start()
            value_copy.start()

            @pl.loop(0, AHEAD)
            def _(g):
                out_copy(g).start()

        @pl.when(t == begin)
        def _():
            key_copy.wait()
            value_copy.wait()
            new_copy.wait_recv()
            new_wide[...] = new[...].astype(F32)

        @pl.when(jnp.logical_and(t >= begin, t < begin + 3))
        def _():
            @pl.loop(0, per)
            def _(i):
                b = (t - begin) * per + i

                @pl.when(b < batches)
                def _():
                    attend(0, b)

        @pl.when(t == begin + 2)
        def _():
            spread_group(0, first_heads)

        @pl.when(jnp.logical_and(t >= LAG, t < chunks + LAG))
        def _():
            c = t - LAG
            slot = c % SLOTS
            wait_bytes(pair_in.at[c], pair_recv.at[c])
            for k, other in enumerate(others):
                line_out[c, k] = encode(mine[slot, other] + decode(pair_in[c, other], shift, 3), shift, 3)
                remote(
                    line_out.at[c, k], line_in.at[c, k], line_send, line_recv.at[c], {"wide": other * 2 + inner}
                ).start()
            kept[slot] = mine[slot, outer] + decode(pair_in[c, outer], shift, 3)

        @pl.when(jnp.logical_and(t >= 2 * LAG, t < chunks + 2 * LAG))
        def _():
            c = t - 2 * LAG
            wait_bytes(line_in.at[c], line_recv.at[c])
            summed = kept[c % SLOTS]
            for k in range(outers - 1):
                summed += decode(line_in[c, k], shift, 3)
            summed = summed.astype(BF16)

            @pl.when(c == 0)
            def _():
                new[half] = summed
                new_copy.start()

            @pl.when(c > 0)
            def _():
                h = c - 1
                query[h // GROUP, :, pl.ds(h % GROUP, 1), :] = summed.astype(F32)[:, None, :]

    early = 0
    if rest_heads:
        early = min(2, first_heads * dh // cols)

        @pl.loop(0, batches)
        def _(b):
            attend(1, b)
            for g in range(early):
                @pl.when(b == (g + 1) * batches // early - 1)
                def _():
                    forward(g)

        spread_group(first_heads, rest_heads)

    def piece_product(g, b):
        count = BLOCK // rows
        left = gathered[g, pl.ds(b * count, count)].reshape(BLOCK, cols)
        return jnp.dot(left, out_weights[g % AHEAD], preferred_element_type=F32)

    def arrive(g):
        wait_bytes(gathered.at[g, pl.ds(0, outers)], spread_pair.at[g])
        wait_bytes(out_weights.at[g % AHEAD], out_sem.at[g % AHEAD])

    total[...] = jnp.zeros_like(total)

    @pl.loop(0, pieces)
    def _(g):
        @pl.when(g >= early)
        def _():
            forward(g)

        @pl.when(g > 0)
        def _():
            arrive(g - 1)

            @pl.loop(0, 2 * blocks)
            def _(b):
                total[b] += piece_product(g - 1, b)

            @pl.when(g - 1 + AHEAD < pieces)
            def _():
                out_copy(g - 1 + AHEAD).start()

    last = pieces - 1
    arrive(last)

    @pl.loop(0, blocks)
    def _(b):
        at = (1 - half) * blocks + b
        half_out[b] = encode(total[at] + piece_product(last, at), 0, 2)
        remote(half_out.at[b], half_in.at[b], half_send, half_recv.at[b], across).start()

    @pl.loop(0, blocks)
    def _(b):
        at = half * blocks + b
        own = total[at] + piece_product(last, at)
        wait_bytes(half_in.at[b], half_recv.at[b])
        result[b] = (own + decode(half_in[b], 0, 2)).astype(BF16)

    pair_tokens.wait_send()
    new_copy.wait_send()
    wait_bytes(pair_out, pair_send)
    wait_bytes(line_out, line_send)
    wait_bytes(gathered.at[:, pl.ds(0, 2 * outers - 1)], spread_send)
    wait_bytes(half_out, half_send)


def shards(wide, tokens, w_query, w_keyval, cache_keys, cache_values, w_out):
    width = tokens.shape[1]
    total_rows = 2 * tokens.shape[0]
    rows, length, dh = cache_keys.shape
    outers = wide // 2
    features = w_query.shape[1]
    heads = features // dh
    chunks = heads + 1
    cols = 2 * dh
    pieces = features // cols
    groups = -(-heads // GROUP)
    blocks = total_rows // 2 // BLOCK
    vmem, dma = pltpu.VMEM, pltpu.SemaphoreType.DMA
    result = pl.pallas_call(
        functools.partial(block_kernel, wide),
        out_shape=jax.ShapeDtypeStruct((blocks, BLOCK, width), BF16),
        in_specs=[pl.BlockSpec(memory_space=pl.ANY)] * 6,
        out_specs=pl.BlockSpec(memory_space=vmem),
        scratch_shapes=[
            vmem((2, total_rows // 2, width), BF16),
            vmem((SLOTS, width, dh), BF16),
            vmem((wide, rows, dh), F32),
            vmem((SLOTS, outers, rows, dh), F32),
            vmem((SLOTS, rows, dh), F32),
            vmem((chunks, outers, rows, dh), BF16),
            vmem((chunks, outers, rows, dh), BF16),
            vmem((chunks, outers - 1, rows, dh), BF16),
            vmem((chunks, outers - 1, rows, dh), BF16),
            vmem((2, rows, dh), BF16),
            vmem((2, rows, dh), F32),
            vmem((groups, rows, GROUP, dh), F32),
            vmem((rows, GROUP, dh), F32),
            vmem((rows, length, dh), BF16),
            vmem((rows, length, dh), BF16),
            vmem((pieces, wide, rows, cols), BF16),
            vmem((AHEAD, cols, width), BF16),
            vmem((2 * blocks, BLOCK, width), F32),
            vmem((blocks, BLOCK, width), BF16),
            vmem((blocks, BLOCK, width), BF16),
            dma((SLOTS,)),
            dma((3,)),
            dma((2,)),
            dma,
            dma((chunks,)),
            dma,
            dma((chunks,)),
            dma((2,)),
            dma((AHEAD,)),
            dma,
            dma((pieces,)),
            dma((pieces,)),
            dma,
            dma((blocks,)),
        ],
        compiler_params=pltpu.CompilerParams(
            collective_id=0, has_side_effects=True, vmem_limit_bytes=62 * 2**20
        ),
        cost_estimate=pl.CostEstimate(
            flops=2 * total_rows * width * (chunks * dh + features),
            bytes_accessed=2 * width * (chunks * dh + features) + 4 * rows * length * dh,
            transcendentals=rows * heads * length,
        ),
    )(tokens, w_query, w_keyval, cache_keys, cache_values, w_out)
    return result.reshape(blocks * BLOCK, width)


def solution(mesh):
    in_specs = (
        P(("groups", "narrow"), "wide"),
        P("wide", "narrow"),
        P("wide", None),
        P(("groups", "wide"), None, None),
        P(("groups", "wide"), None, None),
        P("narrow", "wide"),
    )
    out_specs = P(("groups", "narrow"), "wide")
    return jax.shard_map(
        functools.partial(shards, mesh.shape["wide"]),
        mesh=mesh, in_specs=in_specs, out_specs=out_specs, check_vma=False,
    )
```

time: 314 us -> 125 us (0.40)
  waiting for transfers between devices: 243 us -> 0 us
  Pallas kernels: 0 us -> 123 us
  matrix products: 43.8 us -> 0 us
  between operations: 13.2 us -> 0.01 us
  other arithmetic: 11.5 us -> 0 us
    reduce_scatter x2 -> x0, waiting for transfers between devices: 163 us -> none  [the longest x1 150 us: shards(): lax.psum_scatter(jnp.concatenate([first, second], axis=1), 'wide', scatte...]
    pallas_call x0 -> x1, Pallas kernels: none -> 123 us  [shards(): pl.pallas_call(functools.partial(block_kernel, wide), out_shape=jax.Shape...]
    all_gather x2 -> x0, waiting for transfers between devices: 79.9 us -> none  [the longest x1 64.9 us: shards(): lax.all_gather(mixed, 'wide', axis=0, tiled=True)]
    dot_general x6 -> x0, matrix products: 43.8 us -> none  [the longest x1 15.8 us: shards(): jnp.dot(lax.all_gather(mixed, 'wide', axis=0, tiled=True), w_out, preferr...]
    concatenate x1 -> x0, other arithmetic: 7.03 us -> none  [shards(): jnp.concatenate([first, second], axis=1)]
    convert_element_type x2 -> x0, other arithmetic: 4.07 us -> none  [the longest x1 2.8 us: shards(): return result.astype(jnp.bfloat16)]
  transfers between devices with their start and end apart: 4 -> 0, of which waited for: 4 -> 0; matrix products, arithmetic and copies ran while one was open for 0% -> 0% of each run, Pallas kernels for 0% -> 0%
where the time goes in v2:
time: 125 us
  Pallas kernels  123 us (98%)
  local copies, waits for them, and re-layouts  2.36 us (2%)
    pallas_call x1, Pallas kernels, shards(): pl.pallas_call(functools.partial(block_kernel, wide), out_shape=jax.Shape...  123 us

profile of v2, /device:TPU:1, one launch (start us, length us, event | category | flops | bytes accessed | tf_op | source)
XLA Modules:
  0.0 125.0 jit_solution(13892514174747271138)
XLA Ops:
  0.0 122.6 %shard_map.64 = bf16[2,128,2304]{2,1,0:T(8,128)(2,1)} custom-call(bf16[256,2304]{1,0:T(8,128)(2,1)} %tokens.1, bf16[2304,3584]{1,0:T(8,128)(2,1)} %w_query.1, bf16[2304,512]{1,0:T(8,128)(2,1)} %w_keyval.1, bf16[64,256,256]{2,1,0:T(8,128)(2,1)} %cache_keys.1, bf16[64,256,256]{2,1,0:T(8,128)(2,1)} %cache_values.1, bf16[3584,2304]{1,0:T(8,128)(2,1)} %w_out.1), custom_call_target="tpu_custom_call" | custom-call | flops 17515413504 | bytes 50987008 | tf_op jit(solution)/shard_map/pallas_call | solution.py:318
  122.6 2.4 %copy.8 = bf16[256,2304]{1,0:T(8,128)(2,1)} copy(bf16[256,2304]{1,0:T(8,128)(2,1)} %bitcast.1) | data formatting | bytes 2359296

commit v3 on v2

--- a/solution.py
+++ b/solution.py
@@ -70,7 +70,7 @@
     tok, weights, product, mine, kept, pair_out, pair_in, line_out, line_in, new, new_wide,
     query, mixed, keys, values, gathered, out_weights, total, half_out, half_in,
     w_sem, tok_sem, cache_sem, pair_send, pair_recv, line_send, line_recv, new_sem,
-    out_sem, spread_send, spread_line, spread_pair, half_send, half_recv,
+    out_sem, spread_send, hop_send, hop_recv, spread_pair, half_send, half_recv,
 ):
     outers, me, outer, inner, partner, others = peers(wide)
     half = lax.axis_index("narrow")
@@ -122,10 +122,38 @@
             gathered.at[g, block], gathered.at[g, block], spread_send, recv, {"wide": where}
         ).start()
 
-    def forward(g):
-        wait_bytes(gathered.at[g, pl.ds(0, outers - 1)], spread_line.at[g])
-        for other in others:
-            spread(g, other * 2 + inner, partner, spread_pair.at[g])
+    def may_send(k, up):
+        if up:
+            return jnp.logical_and(outer >= k, outer + 1 < outers)
+        return jnp.logical_and(outer + k < outers, outer >= 1)
+
+    def hop(g, k, up):
+        block = (outer - k if up else outer + k) * 2 + inner
+        where = (outer + 1 if up else outer - 1) * 2 + inner
+        at = (g * (outers - 1) + k) * 2 + up
+        piece = gathered.at[g, block]
+        return remote(piece, piece, hop_send.at[at], hop_recv.at[at], {"wide": where})
+
+    def forward(g, k):
+        for up in (0, 1):
+            source = outer - 1 - k if up else outer + 1 + k
+
+            @pl.when(source >= 0 if up else source < outers)
+            def _():
+                at = (g * (outers - 1) + k) * 2 + up
+                block = source * 2 + inner
+                wait_bytes(gathered.at[g, block], hop_recv.at[at])
+                if k + 1 < outers - 1:
+                    @pl.when(may_send(k + 1, up))
+                    def _():
+                        hop(g, k + 1, up).start()
+                spread(g, block, partner, spread_pair.at[g])
+
+    def forward_step(t):
+        for k in range(outers - 1):
+            @pl.when(jnp.logical_and(t >= k, t - k < pieces))
+            def _():
+                forward(t - k, k)
 
     def attend(group, b):
         take = pl.ds(pl.multiple_of(b * BATCH, BATCH), BATCH)
@@ -152,8 +180,10 @@
             piece, at = divmod((first + j) * dh, cols)
             gathered[piece, me, :, at : at + dh] = mixed[:, j, :].astype(BF16)
         for g in range(first * dh // cols, (first + count) * dh // cols):
-            for other in others:
-                spread(g, me, other * 2 + inner, spread_line.at[g])
+            for up in (0, 1):
+                @pl.when(may_send(0, up))
+                def _():
+                    hop(g, 0, up).start()
             spread(g, me, partner, spread_pair.at[g])
 
     @pl.loop(0, max(chunks + 2 * LAG, begin + 3))
@@ -245,7 +275,7 @@
             for g in range(early):
                 @pl.when(b == (g + 1) * batches // early - 1)
                 def _():
-                    forward(g)
+                    forward_step(g)
 
         spread_group(first_heads, rest_heads)
 
@@ -260,23 +290,24 @@
 
     total[...] = jnp.zeros_like(total)
 
-    @pl.loop(0, pieces)
-    def _(g):
-        @pl.when(g >= early)
-        def _():
-            forward(g)
-
-        @pl.when(g > 0)
-        def _():
-            arrive(g - 1)
+    @pl.loop(0, pieces + outers - 2)
+    def _(t):
+        @pl.when(t >= early)
+        def _():
+            forward_step(t)
+
+        @pl.when(t >= outers - 1)
+        def _():
+            g = t - (outers - 1)
+            arrive(g)
 
             @pl.loop(0, 2 * blocks)
             def _(b):
-                total[b] += piece_product(g - 1, b)
-
-            @pl.when(g - 1 + AHEAD < pieces)
-            def _():
-                out_copy(g - 1 + AHEAD).start()
+                total[b] += piece_product(g, b)
+
+            @pl.when(g + AHEAD < pieces)
+            def _():
+                out_copy(g + AHEAD).start()
 
     last = pieces - 1
     arrive(last)
@@ -298,7 +329,16 @@
     new_copy.wait_send()
     wait_bytes(pair_out, pair_send)
     wait_bytes(line_out, line_send)
-    wait_bytes(gathered.at[:, pl.ds(0, 2 * outers - 1)], spread_send)
+    wait_bytes(gathered.at[:, pl.ds(0, outers)], spread_send)
+
+    @pl.loop(0, pieces)
+    def _(g):
+        for k in range(outers - 1):
+            for up in (0, 1):
+                @pl.when(may_send(k, up))
+                def _():
+                    wait_bytes(gathered.at[g, 0], hop_send.at[(g * (outers - 1) + k) * 2 + up])
+
     wait_bytes(half_out, half_send)
 
 
@@ -351,7 +391,8 @@
             dma((2,)),
             dma((AHEAD,)),
             dma,
-            dma((pieces,)),
+            dma((pieces * (outers - 1) * 2,)),
+            dma((pieces * (outers - 1) * 2,)),
             dma((pieces,)),
             dma,
             dma((blocks,)),

time: 125 us -> 112 us (0.90)
  Pallas kernels: 123 us -> 110 us
    pallas_call x1, Pallas kernels: 123 us -> 110 us  [shards(): pl.pallas_call(functools.partial(block_kernel, wide), out_shape=jax.Shape...]
where the time goes in v3:
time: 112 us
  Pallas kernels  110 us (98%)
  local copies, waits for them, and re-layouts  2.36 us (2%)
    pallas_call x1, Pallas kernels, shards(): pl.pallas_call(functools.partial(block_kernel, wide), out_shape=jax.Shape...  110 us
    unnamed x1, local copies, waits for them, and re-layouts  2.36 us

profile of v3, /device:TPU:1, one launch (start us, length us, event | category | flops | bytes accessed | tf_op | source)
XLA Modules:
  0.0 112.2 jit_solution(16883555500259005178)
XLA Ops:
  0.0 109.8 %shard_map.64 = bf16[2,128,2304]{2,1,0:T(8,128)(2,1)} custom-call(bf16[256,2304]{1,0:T(8,128)(2,1)} %tokens.1, bf16[2304,3584]{1,0:T(8,128)(2,1)} %w_query.1, bf16[2304,512]{1,0:T(8,128)(2,1)} %w_keyval.1, bf16[64,256,256]{2,1,0:T(8,128)(2,1)} %cache_keys.1, bf16[64,256,256]{2,1,0:T(8,128)(2,1)} %cache_values.1, bf16[3584,2304]{1,0:T(8,128)(2,1)} %w_out.1), custom_call_target="tpu_custom_call" | custom-call | flops 17515413504 | bytes 50987008 | tf_op jit(solution)/shard_map/pallas_call | solution.py:358
  109.8 2.4 %copy.8 = bf16[256,2304]{1,0:T(8,128)(2,1)} copy(bf16[256,2304]{1,0:T(8,128)(2,1)} %bitcast.1) | data formatting | bytes 2359296

commit v4 on v3

--- a/solution.py
+++ b/solution.py
@@ -11,7 +11,7 @@
 MESH = pl.DeviceIdType.MESH
 F32 = jnp.float32
 BF16 = jnp.bfloat16
-LAG = 3
+LAG = 2
 SLOTS = LAG + 1
 BLOCK = 128
 GROUP = 8
@@ -398,7 +398,7 @@
             dma((blocks,)),
         ],
         compiler_params=pltpu.CompilerParams(
-            collective_id=0, has_side_effects=True, vmem_limit_bytes=62 * 2**20
+            collective_id=0, has_side_effects=True, vmem_limit_bytes=56 * 2**20
         ),
         cost_estimate=pl.CostEstimate(
             flops=2 * total_rows * width * (chunks * dh + features),

time: 112 us -> 113 us (level)
  no operation moved by 1% of the time
where the time goes in v4:
time: 113 us
  Pallas kernels  111 us (98%)
  local copies, waits for them, and re-layouts  2.36 us (2%)
    pallas_call x1, Pallas kernels, shards(): pl.pallas_call(functools.partial(block_kernel, wide), out_shape=jax.Shape...  111 us
    unnamed x1, local copies, waits for them, and re-layouts  2.36 us

profile of v4, /device:TPU:1, one launch (start us, length us, event | category | flops | bytes accessed | tf_op | source)
XLA Modules:
  0.0 113.1 jit_solution(12672505722598208434)
XLA Ops:
  0.0 110.8 %shard_map.64 = bf16[2,128,2304]{2,1,0:T(8,128)(2,1)} custom-call(bf16[256,2304]{1,0:T(8,128)(2,1)} %tokens.1, bf16[2304,3584]{1,0:T(8,128)(2,1)} %w_query.1, bf16[2304,512]{1,0:T(8,128)(2,1)} %w_keyval.1, bf16[64,256,256]{2,1,0:T(8,128)(2,1)} %cache_keys.1, bf16[64,256,256]{2,1,0:T(8,128)(2,1)} %cache_values.1, bf16[3584,2304]{1,0:T(8,128)(2,1)} %w_out.1), custom_call_target="tpu_custom_call" | custom-call | flops 17515413504 | bytes 50987008 | tf_op jit(solution)/shard_map/pallas_call | solution.py:358
  110.8 2.4 %copy.8 = bf16[256,2304]{1,0:T(8,128)(2,1)} copy(bf16[256,2304]{1,0:T(8,128)(2,1)} %bitcast.1) | data formatting | bytes 2359296
